TPU v7x, 128 devices: a whole 4x4x4 slice. The times are simulated.
128 devices in a mesh: dp: 8 (over y, z_hi), seq: 16 (over z_lo, x, core).
Axes of the slice: x: 4, y: 4, z: 4 (z_hi: 2, z_lo: 2; z = z_hi * 2 + z_lo), core: 2. Of those that a mesh axis runs over, the one named last changes fastest.
Arguments:
- frames: bfloat16 [8, 256, 256, 1280], P('dp', 'seq'), may hold values from -6 to 6
- map_weight: bfloat16 [1280, 8], replicated, may hold values from -0.15625 to 0.15625
- qkv_weight: bfloat16 [1280, 3840], replicated, may hold values from -8 to 8, as said below
- cotangent: bfloat16 [8, 2048, 1280], P('dp', 'seq'), may hold values from -6 to 6
Outputs:
- grad_qkv_weight: float32 [1280, 3840], P(None, 'seq')
Inputs may be any that keep to these rules, and one draw needn't show every extreme that they name: qkv_weight has mean zero and entries of order 1280 ** -0.5 times at most 40.
All inputs are finite; a program needn't handle non-finite values.
Results may differ from a plain program's by a relative error of at most 0.019.
Values may be sent and summed in bfloat16 or wider, within the bound.
No kernel may reach another device: no remote copies, remote signals or barrier semaphores. Data moves between devices by JAX's collectives and lax.ppermute only.
A program may use at most 128 MiB of HBM per device.

v0:
```python
import math
import jax
import jax.numpy as jnp
from jax import lax
from jax.sharding import PartitionSpec as P

HEAD_DIM = 80


def as_sent(array):
    return jax.tree.map(lambda a: a.astype(jnp.bfloat16) if a.dtype == jnp.float32 else a, array)


def learn_tokens(frames, map_weight):
    frame_count = frames.shape[0]
    width_all = frames.shape[2]
    logits = jnp.dot(frames.reshape(-1, width_all), map_weight, preferred_element_type=jnp.float32)
    token_maps = (
        jax.nn.sigmoid(logits).astype(jnp.bfloat16).reshape(frame_count, frames.shape[1], -1)
    )
    pooled = jnp.einsum("fps,fpd->fsd", token_maps, frames, preferred_element_type=jnp.float32)
    pooled = pooled.reshape(-1, width_all)
    centred = pooled - jnp.mean(pooled, axis=-1, keepdims=True)
    variance = jnp.mean(centred * centred, axis=-1, keepdims=True)
    return (centred * lax.rsqrt(variance + 1e-06)).astype(jnp.bfloat16)


def one_head(query_rows, key_rows, value_rows, upstream):
    length = query_rows.shape[0]
    block_rows = math.gcd(length, 512)
    block_count = length // block_rows
    scaling = 1.0 / math.sqrt(HEAD_DIM)

    def advance(totals, position):
        key_total, value_total = totals
        query_block = lax.dynamic_slice_in_dim(query_rows, position * block_rows, block_rows, 0)
        grad_block = lax.dynamic_slice_in_dim(upstream, position * block_rows, block_rows, 0)
        scores = (
            jnp.einsum("qd,kd->qk", query_block, key_rows, preferred_element_type=jnp.float32)
            * scaling
        )
        shifted = jnp.exp(scores - jnp.max(scores, axis=-1, keepdims=True))
        attention = shifted / jnp.sum(shifted, axis=-1, keepdims=True)
        rounded = attention.astype(jnp.bfloat16)
        attended = jnp.dot(rounded, value_rows, preferred_element_type=jnp.float32)
        row_dot = jnp.sum(grad_block.astype(jnp.float32) * attended, axis=-1, keepdims=True)
        grad_attention = jnp.einsum(
            "qd,kd->qk", grad_block, value_rows, preferred_element_type=jnp.float32
        )
        grad_scores = (attention * (grad_attention - row_dot) * scaling).astype(jnp.bfloat16)
        grad_query = jnp.dot(grad_scores, key_rows, preferred_element_type=jnp.float32).astype(
            jnp.bfloat16
        )
        key_total = key_total + jnp.einsum(
            "qk,qd->kd", grad_scores, query_block, preferred_element_type=jnp.float32
        )
        value_total = value_total + jnp.einsum(
            "qk,qd->kd", rounded, grad_block, preferred_element_type=jnp.float32
        )
        return ((key_total, value_total), grad_query)

    empty_rows = jnp.zeros((length, HEAD_DIM), jnp.float32)
    totals, grad_query = lax.scan(advance, (empty_rows, empty_rows), jnp.arange(block_count))
    grad_query = grad_query.reshape(length, HEAD_DIM)
    return jnp.concatenate(
        [grad_query, totals[0].astype(jnp.bfloat16), totals[1].astype(jnp.bfloat16)], axis=1
    )


def heads_backward(projected, upstream):
    query_rows = projected[:, 0:HEAD_DIM]
    key_rows = projected[:, HEAD_DIM : 2 * HEAD_DIM]
    value_rows = projected[:, 2 * HEAD_DIM : 3 * HEAD_DIM]
    pieces = [one_head(query_rows, key_rows, value_rows, upstream)]
    return jnp.concatenate(pieces, axis=1)


def heads_items(operands):
    return jax.vmap(heads_backward)(operands[0], operands[1])


def body(frames, map_weight, qkv_weight, cotangent):
    normed = learn_tokens(frames[0], map_weight)
    projected = jnp.dot(normed, qkv_weight, preferred_element_type=jnp.float32).astype(jnp.bfloat16)
    grads_heads = heads_items(
        (
            lax.all_to_all(projected[None], "seq", split_axis=2, concat_axis=1, tiled=True),
            lax.all_to_all(cotangent, "seq", split_axis=2, concat_axis=1, tiled=True),
        )
    )
    grads = lax.all_to_all(
        as_sent(grads_heads), "seq", split_axis=1, concat_axis=2, tiled=True
    ).astype(grads_heads.dtype)
    partial_value = jnp.einsum("td,tc->dc", normed, grads[0], preferred_element_type=jnp.float32)
    shares = lax.psum_scatter(partial_value, "seq", scatter_dimension=1, tiled=True)
    grad_weight = lax.psum(shares, "dp")
    return grad_weight


def solution(mesh):
    placed = (P("dp", "seq", None, None), P(), P(), P("dp", "seq", None))
    return jax.shard_map(
        body, mesh=mesh, in_specs=placed, out_specs=P(None, "seq"), check_vma=False
    )
```

profile of v0, /device:TPU:0, one launch (start us, length us, event | category | flops | bytes accessed | tf_op | source)
XLA Modules:
  0.0 412.4 jit_solution(12583312983164715362)
XLA Ops:
  6.5 1.4 copy.31
  8.5 7.5 %reduce.9 = bf16[1280,128]{1,0:T(8,128)(2,1)S(1)} reduce(bf16[1280,1,128]{2,1,0:T(2,128)(2,1)S(1)} %bitcast.145, bf16[]{:T(256)} %broadcast.113), dimensions={1}, to_apply=%bitcast.76.reduce_sub_computation | reduce | bytes 655362
  16.8 5.8 %all-to-all-start.1 = ((bf16[16,2,5120]{2,1,0:T(2,128)(2,1)}), bf16[16,2,5120]{2,1,0:T(2,128)(2,1)S(1)}, u32[]{:S(2)}, u32[]{:S(2)}) async-start(bf16[16,2,5120]{2,1,0:T(2,128)(2,1)} %reshape.172), calls=%async_computation.1 | async-start | bytes 655360 | tf_op jit(solution)/shard_map/all_to_all | solution.py:88
  22.7 6.9 %fusion.32 = bf16[4096,8]{0,1:T(8,128)(2,1)S(1)} fusion(bf16[4096,1280]{1,0:T(8,128)(2,1)} %bitcast.134, bf16[1280,8]{0,1:T(8,128)(2,1)S(1)} %copy-done), kind=kOutput, calls=%fused_computation.42 | convolution fusion | flops 84017152 | bytes 10571776 | tf_op jit(solution)/shard_map/dot_general | solution.py:17
  29.6 1.5 fusion.44
  31.6 6.3 %fusion.28 = bf16[1,128,3840]{2,1,0:T(8,128)(2,1)} fusion(bf16[1280,3840]{1,0:T(8,128)(2,1)} %param.8, f32[16,8,1280]{2,1,0:T(8,128)S(1)} %get-tuple-element.160, f32[128]{0:T(128)S(1)} %rsqrt.13, f32[128]{0:T(128)S(1)} %div.23), kind=kOutput, calls=%fused_computation.37 | convolution fusion | flops 1259274240 | bytes 11469824 | tf_op jit(solution)/shard_map/dot_general | solution.py:84
  37.9 3.7 copy.29
  41.5 22.0 %reduce.8 = bf16[3840,128]{1,0:T(8,128)(2,1)} reduce(bf16[3840,1,128]{2,1,0:T(2,128)(2,1)S(1)} %bitcast.137, bf16[]{:T(256)} %broadcast.113), dimensions={1}, to_apply=%bitcast.74.reduce_sub_computation | reduce | bytes 1966082
  63.5 3.1 reshape.170
  67.4 5.7 %all-to-all-start = ((bf16[16,2,15360]{2,1,0:T(2,128)(2,1)}), bf16[16,2,15360]{2,1,0:T(2,128)(2,1)S(1)}, u32[]{:S(2)}, u32[]{:S(2)}) async-start(bf16[16,2,15360]{2,1,0:T(2,128)(2,1)} %reshape.170), calls=%async_computation | async-start | bytes 1966080 | tf_op jit(solution)/shard_map/all_to_all | solution.py:87
  73.4 3.2 reshape.173
  76.7 1.1 copy.43
  77.9 11.0 %all-to-all-done = bf16[16,2,15360]{2,1,0:T(2,128)(2,1)S(1)} async-done(((bf16[16,2,15360]{2,1,0:T(2,128)(2,1)}), bf16[16,2,15360]{2,1,0:T(2,128)(2,1)S(1)}, u32[]{:S(2)}, u32[]{:S(2)}) %all-to-all-start) | async-done | bytes 983072 | tf_op jit(solution)/shard_map/all_to_all | solution.py:87
  88.9 3.2 reshape.171
  92.1 1.7 copy.42
  94.1 0.9 fusion.43
  95.3 1.2 copy.34
  96.5 42.3 %while.17 = (s32[]{:T(128)}, f32[1,2048,80]{1,2,0:T(8,128)S(1)}, f32[1,2048,80]{1,2,0:T(8,128)S(1)}, bf16[4,1,512,80]{2,3,1,0:T(8,128)(2,1)}, s32[4]{0:T(128)S(1...) while((s32[]{:T(128)}, f32[1,2048,80]{1,2,0:T(8,128)S(1)}, ...), condition=%wide.region_6.7_spmd.clone, body=%wide.region_2.6_spmd.clone.sunk | while | flops 1022130688 | bytes 40287472 | solution.py:63
  97.9 1.9 multiply_reduce_fusion.3
  100.6 0.8 fusion.79
  102.9 1.2 multiply_convert_fusion.3
  104.1 1.4 fusion.83
  105.6 1.5 fusion.81
  108.4 1.9 multiply_reduce_fusion.3
  113.4 1.3 multiply_convert_fusion.3
  114.7 1.4 fusion.83
  116.1 1.5 fusion.81
  119.0 1.9 multiply_reduce_fusion.3
  124.0 1.2 multiply_convert_fusion.3
  125.3 1.4 fusion.83
  126.7 1.5 fusion.81
  129.6 1.9 multiply_reduce_fusion.3
  134.6 1.3 multiply_convert_fusion.3
  135.8 1.4 fusion.83
  137.3 1.5 fusion.81
  138.8 1.0 copy.47
  139.9 1.0 pad_maximum_fusion
  140.9 4.6 %copy.37 = bf16[1,2048,240]{2,0,1:T(2,128)(2,1)S(1)} copy(bf16[1,2048,240]{1,2,0:T(8,128)(2,1)} %pad_maximum_fusion) | data formatting | bytes 1966080 | tf_op jit(solution)/shard_map/vmap()/concatenate | solution.py:65
  145.5 12.6 %reduce.10 = bf16[2048,240]{1,0:T(8,128)(2,1)} reduce(bf16[2048,1,240]{2,1,0:T(2,128)(2,1)S(1)} %bitcast.136, bf16[]{:T(256)} %broadcast.113), dimensions={1}, to_apply=%bitcast.78.reduce_sub_computation | reduce | bytes 1966082
  158.2 3.8 reshape.174
  161.9 19.1 %all_to_all.51 = bf16[16,2,15360]{2,1,0:T(2,128)(2,1)} all-to-all(bf16[16,2,15360]{2,1,0:T(2,128)(2,1)S(1)} %reshape.174), channel_id=1, replica_groups=mesh['dp'=8,'seq'=16] {'seq'}, dimensions={0} | all-to-all | bytes 1966080 | tf_op jit(solution)/shard_map/all_to_all | solution.py:91
  181.0 6.0 %reshape.175 = bf16[2048,1,240]{2,1,0:T(2,128)(2,1)S(1)} reshape(bf16[16,2,15360]{2,1,0:T(2,128)(2,1)} %all_to_all.51) | data formatting | bytes 1966080
  187.0 1.2 copy.44
  188.1 1.7 copy.40
  190.1 8.3 %fusion.36 = f32[1280,3840]{0,1:T(8,128)} fusion(bf16[128,3840]{0,1:T(8,128)(2,1)S(1)} %bitcast.140, f32[16,8,1280]{2,1,0:T(8,128)S(1)} %get-tuple-element.160, f32[16,8]{1,0:T(8,128)S(1)} %add_rsqrt_fusion, f32[16,8]{1,0:T(8,128)S(1)} %broadcast_multiply_fusion), kind=kOutput, calls=%fused_computation.51 | convolution fusion | flops 1258782720 | bytes 21300224 | tf_op jit(solution)/shard_map/td,tc->dc/dot_general | solution.py:94
  198.5 112.5 %reduce-scatter.2.cloned.1.call-done = f32[1280,240]{0,1:T(8,128)} async-done(((f32[1280,3840]{0,1:T(8,128)}), f32[1280,240]{0,1:T(8,128)}) %reduce-scatter.2.cloned.1.call-update) | async-done | bytes 1228816 | tf_op jit(solution)/shard_map/reduce_scatter | solution.py:95
  311.0 92.2 %all-reduce.2.cloned.1.call-done = f32[1280,240]{0,1:T(8,128)} async-done(((f32[1280,240]{0,1:T(8,128)}), f32[1280,240]{0,1:T(8,128)}) %all-reduce.2.cloned.1.call-update) | async-done | bytes 1228816 | tf_op jit(solution)/shard_map/psum | solution.py:96
  403.2 2.4 copy.66
  (53 shorter events, 18.1 us)
Async XLA Ops:
  6.5 16.1 %copy-start = (bf16[1280,8]{0,1:T(8,128)(2,1)S(1)}, bf16[1280,8]{0,1:T(8,128)(2,1)}, u32[]{:S(2)}) copy-start(bf16[1280,8]{0,1:T(8,128)(2,1)} %param.7) | copy-start | bytes 61444
  16.8 49.9 %all-to-all-start.1 = ((bf16[16,2,5120]{2,1,0:T(2,128)(2,1)}), bf16[16,2,5120]{2,1,0:T(2,128)(2,1)S(1)}, u32[]{:S(2)}, u32[]{:S(2)}) async-start(bf16[16,2,5120]{2,1,0:T(2,128)(2,1)} %reshape.172), calls=%async_computation.1 | async-start | bytes 655360 | tf_op jit(solution)/shard_map/all_to_all | solution.py:88
  22.7 7.0 %copy-start.2 = (bf16[1,16,256,1280]{3,2,1,0:T(8,128)(2,1)S(1)}, bf16[1,16,256,1280]{3,2,1,0:T(8,128)(2,1)}, u32[]{:S(2)}) copy-start(bf16[1,16,256,1280]{3,2,1,0:T(8,128)(2,1)} %param.6) | copy-start | bytes 31457284
  66.7 0.7 copy-start.3
  67.4 21.5 %all-to-all-start = ((bf16[16,2,15360]{2,1,0:T(2,128)(2,1)}), bf16[16,2,15360]{2,1,0:T(2,128)(2,1)S(1)}, u32[]{:S(2)}, u32[]{:S(2)}) async-start(bf16[16,2,15360]{2,1,0:T(2,128)(2,1)} %reshape.170), calls=%async_computation | async-start | bytes 1966080 | tf_op jit(solution)/shard_map/all_to_all | solution.py:87
  73.1 237.8 %reduce-scatter.2.cloned.1.call-start = ((), (), s32[]{:S(2)}) async-start(), calls=%async_computation.4 | async-start | bytes 20889600 | tf_op jit(solution)/shard_map/reduce_scatter | solution.py:95
  198.4 207.2 %copy-start.1 = (bf16[1280,8]{0,1:T(8,128)(2,1)S(1)}, bf16[1280,8]{0,1:T(8,128)(2,1)}, u32[]{:S(2)}) copy-start(bf16[1280,8]{0,1:T(8,128)(2,1)} %param.7) | copy-start | bytes 61444
  198.4 204.8 %all-reduce.2.cloned.1.call-start = ((), (), s32[]{:S(2)}) async-start(), calls=%async_computation.5 | async-start | bytes 2457600 | tf_op jit(solution)/shard_map/psum | solution.py:96
Sparse Core Ops, SparseCore 0:
  198.5 112.3 reduce-scatter.1
  313.6 89.5 all-reduce.1
where the time goes:
time: 414 us; the launch traced here: 412 us
  waiting for transfers between devices  216 us (52%)
  matrix products  53.1 us (13%)
  other arithmetic  50.4 us (12%)
  local copies, waits for them, and re-layouts  45.7 us (11%)
  blocking collectives  19.1 us (5%)
  between operations  13.6 us (3%)
  starting transfers between devices  11.9 us (3%)
    reduce_scatter x1, waiting for transfers between devices, body(): lax.psum_scatter(partial_value, 'seq', scatter_dimension=1, tiled=True)  112 us
    psum x1, waiting for transfers between devices, body(): grad_weight = lax.psum(shares, 'dp')  92.2 us
    unnamed x5, other arithmetic  42.1 us
    unnamed x22, local copies, waits for them, and re-layouts  30.7 us
    all_to_all x1, blocking collectives, body(): lax.all_to_all(as_sent(grads_heads), 'seq', split_axis=1, concat_axis=2,...  19.1 us
    all_to_all x1, waiting for transfers between devices, body(): lax.all_to_all(projected[None], 'seq', split_axis=2, concat_axis=1, tiled...  11 us
  transfers between devices with their start and end apart: 4, of which 3 were waited for; matrix products, arithmetic and copies ran while one was open for 12% of the time, Pallas kernels for 0%

commit v1 on v0

--- a/solution.py
+++ b/solution.py
@@ -93,7 +93,7 @@
     ).astype(grads_heads.dtype)
     partial_value = jnp.einsum("td,tc->dc", normed, grads[0], preferred_element_type=jnp.float32)
     shares = lax.psum_scatter(partial_value, "seq", scatter_dimension=1, tiled=True)
-    grad_weight = lax.psum(shares, "dp")
+    grad_weight = jnp.sum(lax.all_gather(shares, "dp"), axis=0)
     return grad_weight
 
 

time: 414 us -> 455 us (1.099)
  waiting for transfers between devices: 216 us -> 249 us
    all_gather x0 -> x1, waiting for transfers between devices: none -> 123 us  [body(): grad_weight = jnp.sum(lax.all_gather(shares, 'dp'), axis=0)]
    psum x1 -> x0, waiting for transfers between devices: 92.2 us -> none  [body(): grad_weight = lax.psum(shares, 'dp')]
    unnamed x22 -> x20, local copies, waits for them, and re-layouts: 30.7 us -> 34.1 us
  transfers between devices with their start and end apart: 4 -> 4, of which waited for: 3 -> 3; matrix products, arithmetic and copies ran while one was open for 12% -> 10% of each run, Pallas kernels for 0% -> 0%
where the time goes in v1:
time: 455 us; the launch traced here: 453 us
  waiting for transfers between devices  249 us (55%)
  other arithmetic  54.1 us (12%)
  matrix products  53.1 us (12%)
  local copies, waits for them, and re-layouts  49.2 us (11%)
  blocking collectives  19.1 us (4%)
  between operations  13.6 us (3%)
  starting transfers between devices  12.2 us (3%)
    all_gather x1, waiting for transfers between devices, body(): grad_weight = jnp.sum(lax.all_gather(shares, 'dp'), axis=0)  123 us
    reduce_scatter x1, waiting for transfers between devices, body(): lax.psum_scatter(partial_value, 'seq', scatter_dimension=1, tiled=True)  112 us
    unnamed x5, other arithmetic  42.1 us
    unnamed x20, local copies, waits for them, and re-layouts  34.1 us
    all_to_all x1, blocking collectives, body(): lax.all_to_all(as_sent(grads_heads), 'seq', split_axis=1, concat_axis=2,...  19.1 us
    all_to_all x1, waiting for transfers between devices, body(): lax.all_to_all(projected[None], 'seq', split_axis=2, concat_axis=1, tiled...  13.3 us
  transfers between devices with their start and end apart: 4, of which 3 were waited for; matrix products, arithmetic and copies ran while one was open for 10% of the time, Pallas kernels for 0%

profile of v1, /device:TPU:0, one launch (start us, length us, event | category | flops | bytes accessed | tf_op | source)
XLA Modules:
  0.0 453.0 jit_solution(16971976827845898652)
XLA Ops:
  6.5 1.4 copy.31
  8.5 7.5 %reduce.9 = bf16[1280,128]{1,0:T(8,128)(2,1)S(1)} reduce(bf16[1280,1,128]{2,1,0:T(2,128)(2,1)S(1)} %bitcast.151, bf16[]{:T(256)} %broadcast.113), dimensions={1}, to_apply=%bitcast.81.reduce_sub_computation | reduce | bytes 655362
  16.8 5.8 %all-to-all-start.1 = ((bf16[16,2,5120]{2,1,0:T(2,128)(2,1)}), bf16[16,2,5120]{2,1,0:T(2,128)(2,1)S(1)}, u32[]{:S(2)}, u32[]{:S(2)}) async-start(bf16[16,2,5120]{2,1,0:T(2,128)(2,1)} %reshape.173), calls=%async_computation.1 | async-start | bytes 655360 | tf_op jit(solution)/shard_map/all_to_all | solution.py:88
  22.7 6.9 %fusion.32 = bf16[4096,8]{0,1:T(8,128)(2,1)S(1)} fusion(bf16[4096,1280]{1,0:T(8,128)(2,1)} %bitcast.139, bf16[1280,8]{0,1:T(8,128)(2,1)S(1)} %copy-done), kind=kOutput, calls=%fused_computation.43 | convolution fusion | flops 84017152 | bytes 10571776 | tf_op jit(solution)/shard_map/dot_general | solution.py:17
  29.6 1.5 fusion.44
  31.6 6.3 %fusion.28 = bf16[1,128,3840]{2,1,0:T(8,128)(2,1)} fusion(bf16[1280,3840]{1,0:T(8,128)(2,1)} %param.8, f32[16,8,1280]{2,1,0:T(8,128)S(1)} %get-tuple-element.160, f32[128]{0:T(128)S(1)} %rsqrt.13, f32[128]{0:T(128)S(1)} %div.23), kind=kOutput, calls=%fused_computation.38 | convolution fusion | flops 1259274240 | bytes 11469824 | tf_op jit(solution)/shard_map/dot_general | solution.py:84
  37.9 3.7 copy.29
  41.5 22.0 %reduce.8 = bf16[3840,128]{1,0:T(8,128)(2,1)} reduce(bf16[3840,1,128]{2,1,0:T(2,128)(2,1)S(1)} %bitcast.143, bf16[]{:T(256)} %broadcast.113), dimensions={1}, to_apply=%bitcast.79.reduce_sub_computation | reduce | bytes 1966082
  63.5 3.1 reshape.171
  66.7 5.7 %all-to-all-start = ((bf16[16,2,15360]{2,1,0:T(2,128)(2,1)}), bf16[16,2,15360]{2,1,0:T(2,128)(2,1)S(1)}, u32[]{:S(2)}, u32[]{:S(2)}) async-start(bf16[16,2,15360]{2,1,0:T(2,128)(2,1)} %reshape.171), calls=%async_computation | async-start | bytes 1966080 | tf_op jit(solution)/shard_map/all_to_all | solution.py:87
  72.7 1.0 reshape.174
  73.7 1.1 copy.43
  74.9 13.3 %all-to-all-done = bf16[16,2,15360]{2,1,0:T(2,128)(2,1)S(1)} async-done(((bf16[16,2,15360]{2,1,0:T(2,128)(2,1)}), bf16[16,2,15360]{2,1,0:T(2,128)(2,1)S(1)}, u32[]{:S(2)}, u32[]{:S(2)}) %all-to-all-start) | async-done | bytes 983072 | tf_op jit(solution)/shard_map/all_to_all | solution.py:87
  88.2 3.2 reshape.172
  91.4 1.7 copy.42
  94.3 1.2 copy.35
  95.6 1.2 copy.34
  96.8 42.3 %while.17 = (s32[]{:T(128)}, f32[1,2048,80]{1,2,0:T(8,128)S(1)}, f32[1,2048,80]{1,2,0:T(8,128)S(1)}, bf16[4,1,512,80]{2,3,1,0:T(8,128)(2,1)}, s32[4]{0:T(128)S(1...) while((s32[]{:T(128)}, f32[1,2048,80]{1,2,0:T(8,128)S(1)}, ...), condition=%wide.region_6.7_spmd.clone, body=%wide.region_2.6_spmd.clone.sunk | while | flops 1022130688 | bytes 40287472 | solution.py:63
  98.2 1.9 multiply_reduce_fusion.3
  103.2 1.2 multiply_convert_fusion.3
  104.4 1.4 fusion.83
  105.8 1.5 fusion.81
  108.7 1.9 multiply_reduce_fusion.3
  113.7 1.3 multiply_convert_fusion.3
  115.0 1.4 fusion.83
  116.4 1.5 fusion.81
  119.3 1.9 multiply_reduce_fusion.3
  124.3 1.2 multiply_convert_fusion.3
  125.6 1.4 fusion.83
  127.0 1.5 fusion.81
  129.9 1.9 multiply_reduce_fusion.3
  134.9 1.3 multiply_convert_fusion.3
  136.1 1.4 fusion.83
  137.5 1.5 fusion.81
  139.1 1.0 copy.47
  140.2 1.0 pad_maximum_fusion
  141.2 4.6 %copy.37 = bf16[1,2048,240]{2,0,1:T(2,128)(2,1)S(1)} copy(bf16[1,2048,240]{1,2,0:T(8,128)(2,1)} %pad_maximum_fusion) | data formatting | bytes 1966080 | tf_op jit(solution)/shard_map/vmap()/concatenate | solution.py:65
  145.8 12.6 %reduce.10 = bf16[2048,240]{1,0:T(8,128)(2,1)} reduce(bf16[2048,1,240]{2,1,0:T(2,128)(2,1)S(1)} %bitcast.142, bf16[]{:T(256)} %broadcast.113), dimensions={1}, to_apply=%bitcast.83.reduce_sub_computation | reduce | bytes 1966082
  158.4 3.8 reshape.175
  162.2 19.1 %all_to_all.51 = bf16[16,2,15360]{2,1,0:T(2,128)(2,1)} all-to-all(bf16[16,2,15360]{2,1,0:T(2,128)(2,1)S(1)} %reshape.175), channel_id=1, replica_groups=mesh['dp'=8,'seq'=16] {'seq'}, dimensions={0} | all-to-all | bytes 1966080 | tf_op jit(solution)/shard_map/all_to_all | solution.py:91
  181.3 6.0 %reshape.176 = bf16[2048,1,240]{2,1,0:T(2,128)(2,1)S(1)} reshape(bf16[16,2,15360]{2,1,0:T(2,128)(2,1)} %all_to_all.51) | data formatting | bytes 1966080
  187.2 1.2 copy.44
  188.4 1.7 copy.40
  190.4 8.3 %fusion.36 = f32[1280,3840]{0,1:T(8,128)} fusion(bf16[128,3840]{0,1:T(8,128)(2,1)S(1)} %bitcast.146, f32[16,8,1280]{2,1,0:T(8,128)S(1)} %get-tuple-element.160, f32[16,8]{1,0:T(8,128)S(1)} %add_rsqrt_fusion, f32[16,8]{1,0:T(8,128)S(1)} %broadcast_multiply_fusion), kind=kOutput, calls=%fused_computation.52 | convolution fusion | flops 1258782720 | bytes 21300224 | tf_op jit(solution)/shard_map/td,tc->dc/dot_general | solution.py:94
  199.1 112.2 %reduce-scatter.2.cloned.1.call-done = f32[1280,240]{0,1:T(8,128)} async-done(((f32[1280,3840]{0,1:T(8,128)}), f32[1280,240]{0,1:T(8,128)}) %reduce-scatter.2.cloned.1.call-update) | async-done | bytes 1228816 | tf_op jit(solution)/shard_map/reduce_scatter | solution.py:95
  311.3 123.4 %all-gather.3.cloned.1.call-done = f32[10240,240]{0,1:T(8,128)} async-done(((f32[1280,240]{0,1:T(8,128)}), f32[10240,240]{0,1:T(8,128)}) %all-gather.3.cloned.1.call-update) | async-done | bytes 9830416 | tf_op jit(solution)/shard_map/all_gather | solution.py:96
  434.7 7.8 %copy.48 = f32[30,8,8,1280]{3,2,1,0:T(8,128)S(1)} copy(f32[30,8,8,1280]{3,1,2,0:T(8,128)} %bitcast.140) | data formatting | bytes 19660800
  442.5 3.7 bitcast_reduce_fusion
  (52 shorter events, 19.2 us)
Async XLA Ops:
  6.5 16.1 %copy-start = (bf16[1280,8]{0,1:T(8,128)(2,1)S(1)}, bf16[1280,8]{0,1:T(8,128)(2,1)}, u32[]{:S(2)}) copy-start(bf16[1280,8]{0,1:T(8,128)(2,1)} %param.7) | copy-start | bytes 61444
  16.8 49.9 %all-to-all-start.1 = ((bf16[16,2,5120]{2,1,0:T(2,128)(2,1)}), bf16[16,2,5120]{2,1,0:T(2,128)(2,1)S(1)}, u32[]{:S(2)}, u32[]{:S(2)}) async-start(bf16[16,2,5120]{2,1,0:T(2,128)(2,1)} %reshape.173), calls=%async_computation.1 | async-start | bytes 655360 | tf_op jit(solution)/shard_map/all_to_all | solution.py:88
  22.7 7.0 %copy-start.2 = (bf16[1,16,256,1280]{3,2,1,0:T(8,128)(2,1)S(1)}, bf16[1,16,256,1280]{3,2,1,0:T(8,128)(2,1)}, u32[]{:S(2)}) copy-start(bf16[1,16,256,1280]{3,2,1,0:T(8,128)(2,1)} %param.6) | copy-start | bytes 31457284
  66.7 21.5 %all-to-all-start = ((bf16[16,2,15360]{2,1,0:T(2,128)(2,1)}), bf16[16,2,15360]{2,1,0:T(2,128)(2,1)S(1)}, u32[]{:S(2)}, u32[]{:S(2)}) async-start(bf16[16,2,15360]{2,1,0:T(2,128)(2,1)} %reshape.171), calls=%async_computation | async-start | bytes 1966080 | tf_op jit(solution)/shard_map/all_to_all | solution.py:87
  72.4 238.9 %reduce-scatter.2.cloned.1.call-start = ((), (), s32[]{:S(2)}) async-start(), calls=%async_computation.4 | async-start | bytes 20889600 | tf_op jit(solution)/shard_map/reduce_scatter | solution.py:95
  198.7 236.0 %all-gather.3.cloned.1.call-start = ((), (), s32[]{:S(2)}) async-start(), calls=%async_computation.5 | async-start | bytes 11059200 | tf_op jit(solution)/shard_map/all_gather | solution.py:96
  434.7 11.4 %copy-start.1 = (bf16[1280,8]{0,1:T(8,128)(2,1)S(1)}, bf16[1280,8]{0,1:T(8,128)(2,1)}, u32[]{:S(2)}) copy-start(bf16[1280,8]{0,1:T(8,128)(2,1)} %param.7) | copy-start | bytes 61444
Sparse Core Ops, SparseCore 0:
  198.8 112.3 reduce-scatter.1
  313.8 120.8 all-gather.2
